TPU v7x, 512 devices: a whole 4x8x8 slice. The times are simulated.
512 devices in a mesh: leaf: 32 (over x, z), task: 16 (over y, core).
Axes of the slice: x: 4, y: 8, z: 8, core: 2. Of those that a mesh axis runs over, the one named last changes fastest.
Arguments:
- points: bfloat16 [2097152, 64], P(('leaf', 'task')), may hold values from -6 to 6
- weights: bfloat16 [2097152, 64], P(('leaf', 'task')), may hold values from -4 to 4
- point_order: int32 [32, 16, 4096], P('leaf', 'task'), may hold values from 0 to 4095, each once within a row
- node_order: int32 [32, 16, 4096], P('leaf', 'task'), may hold values from 0 to 4095, each once within a row
- merge_order: int32 [32, 16, 2, 1024], P('leaf', 'task'), may hold values from 0 to 1023, as said below
- far_list: int32 [32, 16, 4, 3], P('leaf', 'task'), may hold values 0 or 1
- task_target: int32 [32, 16, 16, 1], P('leaf', 'task'), may hold values from -1 to 3, as said below
- task_source: int32 [32, 16, 16, 1], P('leaf', 'task'), may hold values from 0 to 3
Outputs:
- potentials: float32 [2097152, 64], P(('leaf', 'task'))
Inputs may be any that keep to these rules, and one draw needn't show every extreme that they name: `merge_order`: each row is a permutation of 0 to 1023; rows [i, j, b] are equal for all i with the same i // 2 ** (b + 1). `task_target`: -1 marks an empty slot; every device of every draw has a slab toward which all 1 slots are used.
All inputs are finite; a program needn't handle non-finite values. No bound on the sum of `far_list` on one device may be relied on, other than what follows from the above.
Results may differ from a plain program's by a relative error of at most 0.002.
Values may be sent and summed in bfloat16 or wider, within the bound.
No kernel may reach another device: no remote copies, remote signals or barrier semaphores. Data moves between devices by JAX's collectives and lax.ppermute only.
A program may use at most 64 MiB of HBM per device.

v0:
```python
import functools
import math

import jax
import jax.numpy as jnp
from jax import lax
from jax.experimental import pallas as pl
from jax.experimental.pallas import tpu as pltpu
from jax.sharding import PartitionSpec as P

LEAF_PTS = 1024
SKEL = 512
LEVELS = 3
LEAF_DEV = 4
F = 64
PTS = LEAF_PTS * LEAF_DEV
RATE = 1.5 / 64 * math.log2(math.e)
VMEM = pl.BlockSpec(memory_space=pltpu.VMEM)
SMEM = pl.BlockSpec(memory_space=pltpu.SMEM)
HBM = pl.BlockSpec(memory_space=pltpu.HBM)
COST = pl.CostEstimate(flops=0, bytes_accessed=1000, transcendentals=0)
PARAMS = pltpu.CompilerParams(vmem_limit_bytes=20 * 2**20)


def split3(value):
    one = value.astype(jnp.bfloat16).astype(jnp.float32)
    rest = value - one
    two = rest.astype(jnp.bfloat16).astype(jnp.float32)
    return one, two, rest - two


def gather_rows(src_ref, index_ref, dst_ref, count, unroll=16):
    def step(i, _):
        for k in range(unroll):
            at = i * unroll + k
            dst_ref[pl.ds(at, 1), :] = src_ref[pl.ds(index_ref[at], 1), :]
        return 0

    lax.fori_loop(0, count // unroll, step, 0)


def sort_kernel(order_ref, points_ref, weights_ref, out_ref, held, arrive, raw, tree):
    copies = []
    for c in range(4):
        cols = pl.ds(c * 1024, 1024)
        for k, array_ref in enumerate((points_ref, weights_ref)):
            into = held.at[pl.ds(k * F, F), cols]
            copies.append(pltpu.make_async_copy(array_ref.at[:, cols], into, arrive.at[2 * c + k]))
    for copy in copies:
        copy.start()
    for c in range(8):
        if c % 2 == 0:
            copies[c].wait()
            copies[c + 1].wait()
        raw[pl.ds(c * 512, 512), :] = held[:, pl.ds(c * 512, 512)].astype(jnp.float32).T
    gather_rows(raw, order_ref, tree, PTS)
    for leaf in range(LEAF_DEV):
        rows = tree[pl.ds(leaf * LEAF_PTS, LEAF_PTS), :]
        out_ref[leaf] = rows.T.astype(jnp.bfloat16)


def sort_leaves(order, points_t, weights_t):
    return pl.pallas_call(
        sort_kernel,
        out_shape=jax.ShapeDtypeStruct((LEAF_DEV, 2 * F, LEAF_PTS), jnp.bfloat16),
        in_specs=[SMEM, HBM, HBM],
        out_specs=VMEM,
        scratch_shapes=[
            pltpu.VMEM((2 * F, PTS), jnp.bfloat16),
            pltpu.SemaphoreType.DMA((8,)),
            pltpu.VMEM((PTS, 2 * F), jnp.float32),
            pltpu.VMEM((PTS, 2 * F), jnp.float32),
        ],
        compiler_params=pltpu.CompilerParams(vmem_limit_bytes=56 * 2**20),
        name="sort_leaves",
        cost_estimate=COST,
    )(order, points_t, weights_t)


def left_factor(rows, with_ones):
    lane = lax.broadcasted_iota(jnp.int32, rows.shape, 1)
    is_point = lane < F
    scaled = jnp.where(is_point, rows * (2 * RATE), 0.0)
    high = scaled.astype(jnp.bfloat16)
    low = scaled - high.astype(jnp.float32)
    norm = -RATE * jnp.sum(jnp.where(is_point, rows * rows, 0.0), axis=1, keepdims=True)
    one, two, three = split3(norm)
    tail = jnp.where(lane == F, one, 0.0)
    tail = jnp.where(lane == F + 1, two, tail)
    tail = jnp.where(lane == F + 2, three, tail)
    if with_ones:
        tail = jnp.where((lane > F + 2) & (lane < F + 6), 1.0, tail)
    second = jnp.where(is_point, low, tail).astype(jnp.bfloat16)
    return jnp.concatenate([high, second], axis=1)


def fill_right(right, block):
    size = block.shape[1]
    points = block[:F]
    wide = points.astype(jnp.float32)
    norm = -RATE * jnp.sum(wide * wide, axis=0, keepdims=True)
    one, two, three = split3(norm)
    row = lax.broadcasted_iota(jnp.int32, (16, size), 0)
    tail = jnp.where(row < 3, 1.0, 0.0)
    tail = jnp.where(row == 3, one, tail)
    tail = jnp.where(row == 4, two, tail)
    tail = jnp.where(row == 5, three, tail)
    right[pl.ds(0, 2 * F), :] = block
    right[pl.ds(2 * F, F), :] = points
    right[pl.ds(3 * F, 16), :] = tail.astype(jnp.bfloat16)
    right[pl.ds(3 * F + 16, F - 16), :] = jnp.zeros((F - 16, size), jnp.bfloat16)


def targets_kernel(leaves_ref, out_ref):
    for leaf in range(LEAF_DEV):
        for half in range(2):
            rows = leaves_ref[leaf, :, pl.ds(half * 512, 512)].astype(jnp.float32).T
            out_ref[pl.ds(leaf * LEAF_PTS + half * 512, 512), :] = left_factor(rows, True)


def target_factors(leaves):
    return pl.pallas_call(
        targets_kernel,
        out_shape=jax.ShapeDtypeStruct((PTS, 4 * F), jnp.bfloat16),
        in_specs=[VMEM],
        out_specs=VMEM,
        compiler_params=PARAMS,
        name="target_factors",
        cost_estimate=COST,
    )(leaves)


def skeleton(index, blocks, right, chosen, total):
    spots = lax.broadcasted_iota(jnp.int32, (SKEL, SKEL), 1).astype(jnp.float32)
    column = jnp.broadcast_to(index, (8, SKEL)).T[:, :1]
    nt = (((1,), (1,)), ((), ()))
    taken = []
    for k, block in enumerate(blocks):
        picks = jnp.where(spots == column - k * SKEL, 1.0, 0.0)
        taken.append(jnp.sum(picks, axis=0, keepdims=True))
        part = lax.dot_general(picks.astype(jnp.bfloat16), block(), nt, preferred_element_type=jnp.float32)
        chosen[...] = part if k == 0 else chosen[...] + part
    left = left_factor(chosen[...], False)
    for k, block in enumerate(blocks):
        rows = block()
        fill_right(right, rows)
        dense = jnp.exp2(jnp.dot(left, right[...], preferred_element_type=jnp.float32))
        factor = jnp.where(taken[k] > 0.5, 0.0, 1.0 / jnp.sum(dense, axis=0, keepdims=True))
        spread = (dense * factor).astype(jnp.bfloat16)
        part = lax.dot_general(spread, rows, nt, preferred_element_type=jnp.float32)
        total[...] = part if k == 0 else total[...] + part
    lane = lax.broadcasted_iota(jnp.int32, (SKEL, 2 * F), 1)
    return (chosen[...] + jnp.where(lane < F, 0.0, total[...])).T.astype(jnp.bfloat16)


SKELETON_SCRATCH = [
    pltpu.VMEM((4 * F, SKEL), jnp.bfloat16),
    pltpu.VMEM((SKEL, 2 * F), jnp.float32),
    pltpu.VMEM((SKEL, 2 * F), jnp.float32),
]


def node_kernel(index_ref, merge_ref, leaves_ref, out_ref, right, chosen, total):
    def block_at(k):
        return lambda: leaves_ref[k // 2, :, pl.ds(k % 2 * SKEL, SKEL)]

    index = index_ref[...].astype(jnp.float32)
    out_ref[pl.ds(0, 2 * F), :] = skeleton(index, [block_at(k) for k in range(2 * LEAF_DEV)], right, chosen, total)
    entry = merge_ref[...]
    high = entry // 32
    row = lax.broadcasted_iota(jnp.int32, (16, SKEL), 0)
    packed = jnp.zeros((16, SKEL), jnp.float32)
    for k, line in enumerate((high[:1], entry[:1] - 32 * high[:1], high[1:2], entry[1:2] - 32 * high[1:2])):
        packed = jnp.where(row == k, line.astype(jnp.float32), packed)
    out_ref[pl.ds(2 * F, 16), :] = packed.astype(jnp.bfloat16)


def first_node(index, merge_index, leaves):
    return pl.pallas_call(
        node_kernel,
        out_shape=jax.ShapeDtypeStruct((2 * F + 16, SKEL), jnp.bfloat16),
        in_specs=[VMEM, VMEM, VMEM],
        out_specs=VMEM,
        scratch_shapes=SKELETON_SCRATCH,
        compiler_params=PARAMS,
        name="first_node",
        cost_estimate=COST,
    )(index, merge_index, leaves)


def add_terms(target, block, left_ref, total, right):
    fill_right(right, block)
    weights = block
    base = pl.multiple_of(target * LEAF_PTS, LEAF_PTS)
    for step in range(LEAF_PTS // 256):
        rows = pl.ds(base + step * 256, 256)
        exponent = jnp.dot(left_ref[rows, :], right[...], preferred_element_type=jnp.float32)
        dense = jnp.exp2(exponent).astype(jnp.bfloat16)
        total[rows, :] += lax.dot_general(
            dense, weights, (((1,), (1,)), ((), ())), preferred_element_type=jnp.float32
        )


def far_kernel(place_ref, flags_ref, left_ref, before_ref, nodes_ref, out_ref, siblings, pairs, arrive, right, chosen, total):
    fetch = pltpu.make_async_copy(before_ref, out_ref, arrive)
    fetch.start()
    place = place_ref[0]
    pair = place // 2
    quad = place // 4
    other_pair = pair + 1 - 2 * (pair % 2)
    other_quad = quad + 1 - 2 * (quad % 2)
    siblings[0] = nodes_ref[place + 1 - 2 * (place % 2), pl.ds(0, 2 * F), :]

    def entries(base, level):
        lines = nodes_ref[base, pl.ds(2 * F, 16), :].astype(jnp.float32)
        return lines[2 * level : 2 * level + 1] * 32.0 + lines[2 * level + 1 : 2 * level + 2]

    def merge_pair(k, _):
        base = 2 * jnp.where(k == 0, other_pair, 2 * other_quad + k - 1)
        blocks = [lambda: nodes_ref[base, pl.ds(0, 2 * F), :], lambda: nodes_ref[base + 1, pl.ds(0, 2 * F), :]]
        pairs[k] = skeleton(entries(base, 0), blocks, right, chosen, total)
        return 0

    lax.fori_loop(0, 3, merge_pair, 0)
    siblings[1] = pairs[0]
    siblings[2] = skeleton(entries(4 * other_quad, 1), [lambda: pairs[1], lambda: pairs[2]], right, chosen, total)
    fetch.wait()
    for level in range(LEVELS):
        block = siblings[level]
        fill_right(right, block)

        def leaf_step(leaf, _):
            @pl.when(flags_ref[leaf * LEVELS + level] != 0)
            def _():
                base = pl.multiple_of(leaf * LEAF_PTS, LEAF_PTS)
                for step in range(2):
                    rows = pl.ds(base + step * 512, 512)
                    exponent = jnp.dot(left_ref[rows, :], right[...], preferred_element_type=jnp.float32)
                    dense = jnp.exp2(exponent).astype(jnp.bfloat16)
                    out_ref[rows, :] += lax.dot_general(
                        dense, block, (((1,), (1,)), ((), ())), preferred_element_type=jnp.float32
                    )
            return 0

        lax.fori_loop(0, LEAF_DEV, leaf_step, 0)


def far_terms(place, flags, left, before, nodes):
    return pl.pallas_call(
        far_kernel,
        out_shape=jax.ShapeDtypeStruct((PTS, 2 * F), jnp.float32),
        in_specs=[SMEM, SMEM, VMEM, HBM, VMEM],
        out_specs=VMEM,
        scratch_shapes=[
            pltpu.VMEM((3, 2 * F, SKEL), jnp.bfloat16),
            pltpu.VMEM((3, 2 * F, SKEL), jnp.bfloat16),
            pltpu.SemaphoreType.DMA,
            *SKELETON_SCRATCH,
        ],
        compiler_params=PARAMS,
        name="far_terms",
        cost_estimate=COST,
    )(place, flags, left, before, nodes)


def source_of(me, distance, other):
    core = me % 2
    chip = (me // 2 - (1 - 2 * core) * distance + 8) % 8
    return 2 * chip + (core + other) % 2


def copy_kernel(picks, me_ref, table_ref, *refs):
    inputs, outputs, arrive = refs[: -1 - len(picks)], refs[-1 - len(picks) : -1], refs[-1]
    me = me_ref[0]
    rows = [(out_ref, k, *pick) for out_ref, out in zip(outputs, picks) for k, pick in enumerate(out)]
    copies = [
        pltpu.make_async_copy(inputs[source].at[leaf_of(me, table_ref)], out_ref.at[k], arrive.at[at])
        for at, (out_ref, k, source, leaf_of) in enumerate(rows)
    ]
    for copy in copies:
        copy.start()
    for copy in copies:
        copy.wait()


def copy_leaves(me, table, inputs, picks):
    size = (2 * F, LEAF_PTS)
    return pl.pallas_call(
        functools.partial(copy_kernel, picks),
        out_shape=[jax.ShapeDtypeStruct((len(rows),) + size, jnp.bfloat16) for rows in picks],
        in_specs=[SMEM, SMEM] + [HBM] * len(inputs),
        out_specs=[VMEM] * len(picks),
        scratch_shapes=[pltpu.SemaphoreType.DMA((sum(len(rows) for rows in picks),))],
        compiler_params=PARAMS,
        name="copy_leaves",
        cost_estimate=COST,
    )(me, table, *inputs)


def asked(distance, other, to_chip, to_other):
    def leaf_of(me, table_ref):
        core = me % 2
        chip = (me // 2 + (1 - 2 * core) * to_chip + 8) % 8
        return table_ref[2 * chip + (core + to_other) % 2, 0, source_of(me, distance, other)]

    return leaf_of


def at_slot(slot):
    return lambda me, table_ref: slot


def near_kernel(items, first, last, me_ref, source_ref, target_ref, left_ref, *refs):
    refs = list(refs)
    before_ref = None if first else refs.pop(0)
    count = len(items)
    arrays, out_ref, held, arrive, right = refs[:count], refs[count], refs[count + 1], refs[count + 2], refs[count + 3]
    total = refs[count + 4] if last else out_ref
    plan = []
    for k, ((distance, other, slot), array_ref) in enumerate(zip(items, arrays)):
        peer = source_of(me_ref[0], distance, other)
        leaf = source_ref[peer] if slot is None else slot
        plan.append((target_ref[peer], pltpu.make_async_copy(array_ref.at[leaf], held.at[k], arrive.at[k])))
    for target, copy in plan:
        pl.when(target >= 0)(copy.start)
    total[...] = jnp.zeros_like(total) if first else before_ref[...]
    for k, (target, copy) in enumerate(plan):

        @pl.when(target >= 0)
        def _():
            copy.wait()
            add_terms(target, held[k], left_ref, total, right)

    if last:
        for part in range(8):
            rows = pl.ds(part * 512, 512)
            out_ref[:, rows] = total[rows, :].T[F:]


def near_terms(me, source, target, left, before, items, last=False):
    first = before is None
    plan = [item[1:] for item in items]
    count = len(items)
    scratch = [
        pltpu.VMEM((count, 2 * F, LEAF_PTS), jnp.bfloat16),
        pltpu.SemaphoreType.DMA((count,)),
        pltpu.VMEM((4 * F, LEAF_PTS), jnp.bfloat16),
    ]
    if last:
        scratch.append(pltpu.VMEM((PTS, 2 * F), jnp.float32))
    return pl.pallas_call(
        functools.partial(near_kernel, plan, first, last),
        out_shape=jax.ShapeDtypeStruct((F, PTS) if last else (PTS, 2 * F), jnp.float32),
        in_specs=[SMEM] * 3 + [VMEM] * (1 if first else 2) + [HBM] * count,
        out_specs=VMEM,
        scratch_shapes=scratch,
        compiler_params=PARAMS,
        name="near_terms",
        cost_estimate=COST,
    )(me, source, target, left, *([] if first else [before]), *[item[0] for item in items])


def partner(value, axis, stride):
    pairs = [(source, source ^ 2**stride) for source in range(lax.axis_size(axis))]
    return lax.ppermute(value, axis, pairs)


def hop(value):
    pairs = [(j, (j + 2 - 4 * (j % 2)) % 16) for j in range(16)]
    return lax.ppermute(value, "task", pairs)


def after(value, *others):
    return lax.optimization_barrier((value, *others))[0]


def body(points, weights, point_order, node_order, merge_order, far_list, task_target, task_source):
    me = lax.axis_index("task").astype(jnp.int32).reshape(1)
    source = task_source.reshape(-1)
    target = task_target.reshape(-1)
    near = functools.partial(near_terms, me, source, target)
    place = (lax.axis_index("leaf") % 8).astype(jnp.int32).reshape(1)

    row = jnp.broadcast_to(source, (16, 1, 16))
    table = lax.all_to_all(row, "task", split_axis=0, concat_axis=0, tiled=True)
    leaves = after(sort_leaves(point_order.reshape(-1), points.T, weights.T), table)
    one_a = hop(leaves)
    beside = partner(leaves, "task", 0)
    one_b = hop(beside)
    left = target_factors(after(leaves, beside))
    node = first_node(node_order.reshape(1, -1)[:, :SKEL], merge_order[0, 0, :, :SKEL], after(leaves, beside))
    groups = [list(range(8 * x, 8 * x + 8)) for x in range(lax.axis_size("leaf") // 8)]
    nodes = lax.all_to_all(
        jnp.broadcast_to(node, (8,) + node.shape), "leaf", split_axis=0, concat_axis=0, axis_index_groups=groups, tiled=True
    )

    one_a = after(one_a, node)
    two_a = hop(one_a)
    one_b = after(one_b, one_a)
    two_b = hop(one_b)
    total = near(
        left,
        None,
        [
            (leaves, 0, 0, None),
            (beside, 0, 1, None),
            (one_a, 1, 0, None),
            (one_b, 1, 1, None),
        ],
    )
    two_a = after(two_a, total)
    send, send_side = copy_leaves(
        me,
        table,
        [one_a, one_b, two_a],
        [
            [(2, asked(2, 0, 1, 0)), (2, asked(2, 0, 1, 1)), (2, asked(2, 0, 2, 0))],
            [(0, asked(1, 0, 0, 1)), (1, asked(1, 1, 0, 1)), (2, asked(2, 0, 0, 1))],
        ],
    )
    three_a = hop(send)
    side = partner(send_side, "task", 0)
    two_b = after(two_b, send)
    [send] = copy_leaves(
        me, table, [two_b], [[(0, asked(2, 1, 1, 0)), (0, asked(2, 1, 1, 1)), (0, asked(2, 1, 2, 0))]]
    )
    three_b = hop(send)
    total = far_terms(place, far_list.reshape(-1), left, total, after(nodes, send))
    three_a = after(three_a, total)
    send, send_side = copy_leaves(
        me,
        table,
        [two_b, three_a, three_b],
        [[(1, at_slot(2)), (2, at_slot(2))], [(0, asked(2, 1, 0, 1)), (1, at_slot(1)), (2, at_slot(1))]],
    )
    four = hop(send)
    last_side = partner(send_side, "task", 0)
    total = near(
        left,
        total,
        [
            (after(two_a, send), 2, 0, None),
            (two_b, 2, 1, None),
            (side, -1, 1, 0),
            (side, -1, 0, 1),
            (side, -2, 1, 2),
            (three_a, 3, 0, 0),
            (three_b, 3, 1, 0),
        ],
    )
    last_side = after(last_side, total)
    total = near(
        left,
        total,
        [
            (last_side, -2, 0, 0),
            (last_side, -3, 1, 1),
            (last_side, -3, 0, 2),
            (after(four, last_side), 4, 0, 0),
            (four, 4, 1, 1),
        ],
        last=True,
    )
    return total.T


def solution(mesh):
    return jax.shard_map(
        body,
        mesh=mesh,
        in_specs=(
            P(("leaf", "task"), None),
            P(("leaf", "task"), None),
            P("leaf", "task", None),
            P("leaf", "task", None),
            P("leaf", "task", None, None),
            P("leaf", "task", None, None),
            P("leaf", "task", None, None),
            P("leaf", "task", None, None),
        ),
        out_specs=P(("leaf", "task"), None),
        check_vma=False,
    )
```

profile of v0, /device:TPU:22, one launch (start us, length us, event | category | flops | bytes accessed | tf_op | source)
XLA Modules:
  0.0 125.7 jit_solution(14498133067268455577)
XLA Ops:
  0.0 1.3 %broadcast_in_dim.6 = s32[16,1,16]{2,1,0:T(1,128)} broadcast(s32[16]{0:T(128)} %bitcast.11), dimensions={2} | broadcast | bytes 1088 | tf_op jit(solution)/shard_map/broadcast_in_dim | solution.py:384
  1.3 7.5 %all-to-all-start = ((s32[16,1,16]{2,1,0:T(1,128)}), s32[16,1,16]{2,1,0:T(1,128)S(1)}, u32[]{:S(2)}, u32[]{:S(2)}) async-start(s32[16,1,16]{2,1,0:T(1,128)} %broadcast_in_dim.6), calls=%async_computation | async-start | bytes 16384 | tf_op jit(solution)/shard_map/all_to_all | solution.py:385
  8.7 8.3 %sort_leaves.1.leaves_ref.refs_0_ = bf16[4,128,1024]{2,1,0:T(8,128)(2,1)} custom-call(s32[4096]{0:T(1024)} %bitcast.20, bf16[64,4096]{1,0:T(8,128)(2,1)} %bitcast.18, bf16[64,4096]{1,0:T(8,128)(2,1)} %bitcast.19), custom_call_target="tpu_custom_call" | custom-call | bytes 1000 | tf_op jit(solution)/shard_map/sort_leaves/pallas_call | solution.py:63
  17.0 2.1 %collective-permute-start = (bf16[4,128,1024]{2,1,0:T(8,128)(2,1)}, bf16[4,128,1024]{2,1,0:T(8,128)(2,1)S(1)}, u32[]{:S(2)}, u32[]{:S(2)}) collective-permute-start(bf16[4,128,1024]{2,1,0:T(8,128)(2,1)} %sort_leaves.1.leaves_ref.refs_0_), channel_id=1, source_target_pairs={{0,1},{1,0},{2,3},{3,2},{4,5},{5,4},{6,7},{7,6},{8,9},{9,8},{10,11... | collective-permute-start | bytes 3145736 | tf_op jit(solution)/shard_map/ppermute | solution.py:365
  19.1 3.4 %collective-permute-start.1 = (bf16[4,128,1024]{2,1,0:T(8,128)(2,1)}, bf16[4,128,1024]{2,1,0:T(8,128)(2,1)}, u32[]{:S(2)}, u32[]{:S(2)}) collective-permute-start(bf16[4,128,1024]{2,1,0:T(8,128)(2,1)} %sort_leaves.1.leaves_ref.refs_0_), channel_id=1, source_target_pairs={{0,2},{1,15},{2,4},{3,1},{4,6},{5,3},{6,8},{7,5},{8,10},{9,7},{10,... | collective-permute-start | bytes 3145736 | tf_op jit(solution)/shard_map/ppermute | solution.py:370
  22.5 4.6 %collective-permute-start.2 = (bf16[4,128,1024]{2,1,0:T(8,128)(2,1)S(1)}, bf16[4,128,1024]{2,1,0:T(8,128)(2,1)}, u32[]{:S(2)}, u32[]{:S(2)}) collective-permute-start(bf16[4,128,1024]{2,1,0:T(8,128)(2,1)S(1)} %collective-permute-done.refs_1_), channel_id=1, source_target_pairs={{0,2},{1,15},{2,4},{3,1},{4,6},{5,3},{6,8},{7,5},{8,10},{9,7},{10,... | collective-permute-start | bytes 3145736 | tf_op jit(solution)/shard_map/ppermute | solution.py:370
  27.1 0.7 slice.8.index_ref
  27.8 1.2 copy-done
  29.0 6.2 %first_node.1 = bf16[144,512]{1,0:T(8,128)(2,1)S(1)} custom-call(s32[1,512]{1,0:T(1,128)S(1)} %slice.8.index_ref, s32[2,512]{1,0:T(2,128)S(1)} %slice_bitcast_fusion.merge_ref, bf16[4,128,1024]{2,1,0:T(8,128)(2,1)S(1)} %copy-done), custom_call_target="tpu_custom_call" | custom-call | bytes 1000 | tf_op jit(solution)/shard_map/first_node/pallas_call | solution.py:179
  35.2 1.1 broadcast_in_dim.7
  36.4 10.3 %all-to-all-start.1 = ((bf16[8,144,512]{2,1,0:T(8,128)(2,1)}), bf16[8,144,512]{2,1,0:T(8,128)(2,1)}, u32[]{:S(2)}, u32[]{:S(2)}) async-start(bf16[8,144,512]{2,1,0:T(8,128)(2,1)} %broadcast_in_dim.7), calls=%async_computation.1 | async-start | bytes 2359296 | tf_op jit(solution)/shard_map/all_to_all | solution.py:393
  46.7 2.7 %collective-permute-start.4 = (bf16[4,128,1024]{2,1,0:T(8,128)(2,1)}, bf16[4,128,1024]{2,1,0:T(8,128)(2,1)}, u32[]{:S(2)}, u32[]{:S(2)}) collective-permute-start(bf16[4,128,1024]{2,1,0:T(8,128)(2,1)} %collective-permute-done.1.refs_2_.refs_0_), channel_id=1, source_target_pairs={{0,2},{1,15},{2,4},{3,1},{4,6},{5,3},{6,8},{7,5},{8,10},{9,7},{10,... | collective-permute-start | bytes 3145736 | tf_op jit(solution)/shard_map/ppermute | solution.py:370
  49.4 2.5 %collective-permute-start.3 = (bf16[4,128,1024]{2,1,0:T(8,128)(2,1)}, bf16[4,128,1024]{2,1,0:T(8,128)(2,1)}, u32[]{:S(2)}, u32[]{:S(2)}) collective-permute-start(bf16[4,128,1024]{2,1,0:T(8,128)(2,1)} %collective-permute-done.2.refs_3_.refs_1_), channel_id=1, source_target_pairs={{0,2},{1,15},{2,4},{3,1},{4,6},{5,3},{6,8},{7,5},{8,10},{9,7},{10,... | collective-permute-start | bytes 3145736 | tf_op jit(solution)/shard_map/ppermute | solution.py:370
  51.9 1.6 %target_factors.1.left_ref = bf16[4096,256]{1,0:T(8,128)(2,1)S(1)} custom-call(bf16[4,128,1024]{2,1,0:T(8,128)(2,1)S(1)} %copy-done.1), custom_call_target="tpu_custom_call" | custom-call | bytes 1000 | tf_op jit(solution)/shard_map/target_factors/pallas_call | solution.py:122
  53.5 2.2 %near_terms.3.before_ref = f32[4096,128]{1,0:T(8,128)S(1)} custom-call(s32[1]{0:T(128)} %bitcast.me_ref, s32[16]{0:T(128)S(1)} %bitcast.12, s32[16]{0:T(128)S(1)} %bitcast.15, bf16[4096,256]{1,0:T(8,128)(2,1)S(1)} %target_factors.1.left_ref, bf16[4,128,1024]{2,1,0:T(8,128)(2,1)S(1)} %copy-done.1, bf16[4,128,1024]{2,1,0:T(8,128)(2,1)S(1)} %copy-done.5, ...), custom_call_target="tpu_custom_call" | custom-call | bytes 1000 | tf_op jit(solution)/shard_map/near_terms/pallas_call | solution.py:351
  55.7 1.3 %copy-done.2 = f32[4096,128]{1,0:T(8,128)} copy-done((f32[4096,128]{1,0:T(8,128)}, f32[4096,128]{1,0:T(8,128)S(1)}, u32[]{:S(2)}) %copy-start.2) | copy-done | bytes 2097176
  57.1 6.7 %collective-permute-done.4.refs_2_.refs_1_ = bf16[4,128,1024]{2,1,0:T(8,128)(2,1)} collective-permute-done((bf16[4,128,1024]{2,1,0:T(8,128)(2,1)}, bf16[4,128,1024]{2,1,0:T(8,128)(2,1)}, u32[]{:S(2)}, u32[]{:S(2)}) %collective-permute-start.4) | collective-permute-done | bytes 1048608 | tf_op jit(solution)/shard_map/ppermute | solution.py:370
  63.7 3.0 %copy_leaves.3 = (bf16[3,128,1024]{2,1,0:T(8,128)(2,1)}, bf16[3,128,1024]{2,1,0:T(8,128)(2,1)S(1)}) custom-call(s32[1]{0:T(128)} %bitcast.me_ref, s32[16,1,16]{2,1,0:T(1,128)S(1)} %all-to-all-done.table_ref, bf16[4,128,1024]{2,1,0:T(8,128)(2,1)} %collective-permute-done.1.refs_2_.refs_0_, bf16[4,128,1024]{2,1,0:T(8,128)(2,1)} %collective-permute-done.2.refs_3_.refs_1_, ...), custom_call_target="tpu_custom_call" | custom-call | bytes 1000 | tf_op jit(solution)/shard_map/copy_leaves/pallas_call | solution.py:288
  66.7 1.0 copy-done.8
  67.7 2.6 %collective-permute-start.5 = (bf16[3,128,1024]{2,1,0:T(8,128)(2,1)}, bf16[3,128,1024]{2,1,0:T(8,128)(2,1)}, u32[]{:S(2)}, u32[]{:S(2)}) collective-permute-start(bf16[3,128,1024]{2,1,0:T(8,128)(2,1)} %get-tuple-element.25), channel_id=1, source_target_pairs={{0,2},{1,15},{2,4},{3,1},{4,6},{5,3},{6,8},{7,5},{8,10},{9,7},{10,... | collective-permute-start | bytes 2359304 | tf_op jit(solution)/shard_map/ppermute | solution.py:370
  70.3 4.6 %collective-permute-done.3.refs_0_.refs_2_ = bf16[4,128,1024]{2,1,0:T(8,128)(2,1)} collective-permute-done((bf16[4,128,1024]{2,1,0:T(8,128)(2,1)}, bf16[4,128,1024]{2,1,0:T(8,128)(2,1)}, u32[]{:S(2)}, u32[]{:S(2)}) %collective-permute-start.3) | collective-permute-done | bytes 1048608 | tf_op jit(solution)/shard_map/ppermute | solution.py:370
  75.0 2.7 %copy_leaves.4 = bf16[3,128,1024]{2,1,0:T(8,128)(2,1)} custom-call(s32[1]{0:T(128)} %bitcast.me_ref, s32[16,1,16]{2,1,0:T(1,128)S(1)} %all-to-all-done.table_ref, bf16[4,128,1024]{2,1,0:T(8,128)(2,1)} %collective-permute-done.3.refs_0_.refs_2_), custom_call_target="tpu_custom_call" | custom-call | bytes 1000 | tf_op jit(solution)/shard_map/copy_leaves/pallas_call | solution.py:288
  77.7 2.7 %collective-permute-start.6 = (bf16[3,128,1024]{2,1,0:T(8,128)(2,1)}, bf16[3,128,1024]{2,1,0:T(8,128)(2,1)}, u32[]{:S(2)}, u32[]{:S(2)}) collective-permute-start(bf16[3,128,1024]{2,1,0:T(8,128)(2,1)} %copy_leaves.4), channel_id=1, source_target_pairs={{0,2},{1,15},{2,4},{3,1},{4,6},{5,3},{6,8},{7,5},{8,10},{9,7},{10,... | collective-permute-start | bytes 2359304 | tf_op jit(solution)/shard_map/ppermute | solution.py:370
  80.4 0.1 copy.10
  80.6 1.9 %collective-permute-start.7 = (bf16[3,128,1024]{2,1,0:T(8,128)(2,1)}, bf16[3,128,1024]{2,1,0:T(8,128)(2,1)S(1)}, u32[]{:S(2)}, u32[]{:S(2)}) collective-permute-start(bf16[3,128,1024]{2,1,0:T(8,128)(2,1)} %copy-done.8), channel_id=1, source_target_pairs={{0,1},{1,0},{2,3},{3,2},{4,5},{5,4},{6,7},{7,6},{8,9},{9,8},{10,11... | collective-permute-start | bytes 2359304 | tf_op jit(solution)/shard_map/ppermute | solution.py:365
  82.5 1.6 %copy-done.3 = f32[4096,128]{1,0:T(8,128)S(1)} copy-done((f32[4096,128]{1,0:T(8,128)S(1)}, f32[4096,128]{1,0:T(8,128)}, u32[]{:S(2)}) %copy-start.3) | copy-done | bytes 2097176
  84.1 14.9 %far_terms.1.refs_0_ = f32[4096,128]{1,0:T(8,128)S(1)} custom-call(s32[1]{0:T(128)} %bitcast.6.place_ref, s32[12]{0:T(128)S(1)} %reshape.26.flags_ref, bf16[4096,256]{1,0:T(8,128)(2,1)S(1)} %target_factors.1.left_ref, f32[4096,128]{1,0:T(8,128)S(1)} %copy-done.3, bf16[8,144,512]{2,1,0:T(8,128)(2,1)} %all-to-all-done.1.nodes_ref), custom_call_target="tpu_custom_call" | custom-call | bytes 1000 | tf_op jit(solution)/shard_map/far_terms/pallas_call | solution.py:249
  99.0 2.0 %copy_leaves.5 = (bf16[2,128,1024]{2,1,0:T(8,128)(2,1)S(1)}, bf16[3,128,1024]{2,1,0:T(8,128)(2,1)S(1)}) custom-call(s32[1]{0:T(128)} %bitcast.me_ref, s32[16,1,16]{2,1,0:T(1,128)S(1)} %all-to-all-done.table_ref, bf16[4,128,1024]{2,1,0:T(8,128)(2,1)} %collective-permute-done.3.refs_0_.refs_2_, bf16[3,128,1024]{2,1,0:T(8,128)(2,1)} %collective-permute-done.5.refs_1_.refs_6_, ...), custom_call_target="tpu_custom_call" | custom-call | bytes 1000 | tf_op jit(solution)/shard_map/copy_leaves/pallas_call | solution.py:288
  101.0 5.2 %collective-permute-start.8 = (bf16[3,128,1024]{2,1,0:T(8,128)(2,1)S(1)}, bf16[3,128,1024]{2,1,0:T(8,128)(2,1)S(1)}, u32[]{:S(2)}, u32[]{:S(2)}) collective-permute-start(bf16[3,128,1024]{2,1,0:T(8,128)(2,1)S(1)} %get-tuple-element.32), channel_id=1, source_target_pairs={{0,1},{1,0},{2,3},{3,2},{4,5},{5,4},{6,7},{7,6},{8,9},{9,8},{10,11... | collective-permute-start | bytes 2359304 | tf_op jit(solution)/shard_map/ppermute | solution.py:365
  106.2 3.7 %collective-permute-start.9 = (bf16[2,128,1024]{2,1,0:T(8,128)(2,1)S(1)}, bf16[2,128,1024]{2,1,0:T(8,128)(2,1)S(1)}, u32[]{:S(2)}, u32[]{:S(2)}) collective-permute-start(bf16[2,128,1024]{2,1,0:T(8,128)(2,1)S(1)} %get-tuple-element.29), channel_id=1, source_target_pairs={{0,2},{1,15},{2,4},{3,1},{4,6},{5,3},{6,8},{7,5},{8,10},{9,7},{10,... | collective-permute-start | bytes 1572872 | tf_op jit(solution)/shard_map/ppermute | solution.py:370
  109.9 8.1 %near_terms.4.refs_0_ = f32[4096,128]{1,0:T(8,128)S(1)} custom-call(s32[1]{0:T(128)} %bitcast.me_ref, s32[16]{0:T(128)S(1)} %bitcast.13, s32[16]{0:T(128)S(1)} %bitcast.16, bf16[4096,256]{1,0:T(8,128)(2,1)S(1)} %target_factors.1.left_ref, f32[4096,128]{1,0:T(8,128)S(1)} %far_terms.1.refs_0_, bf16[4,128,1024]{2,1,0:T(8,128)(2,1)} %collective-permute-done.4.refs_2_.refs_1_, ...), custom_call_target="tpu_custom_call" | custom-call | bytes 1000 | tf_op jit(solution)/shard_map/near_terms/pallas_call | solution.py:351
  118.0 7.5 %near_terms.5 = f32[64,4096]{1,0:T(8,128)} custom-call(s32[1]{0:T(128)} %bitcast.me_ref, s32[16]{0:T(128)S(1)} %bitcast.14, s32[16]{0:T(128)S(1)} %bitcast.17, bf16[4096,256]{1,0:T(8,128)(2,1)S(1)} %target_factors.1.left_ref, f32[4096,128]{1,0:T(8,128)S(1)} %near_terms.4.refs_0_, bf16[3,128,1024]{2,1,0:T(8,128)(2,1)S(1)} %collective-permute-done.8.refs_1_.refs_2_.refs_3_, ...), custom_call_target="tpu_custom_call" | custom-call | bytes 1000 | tf_op jit(solution)/shard_map/near_terms/pallas_call | solution.py:351
  (30 shorter events, 0.2 us)
Async XLA Ops:
  0.0 27.8 %copy-start.9 = (s32[1,1,2,1024]{3,2,1,0:T(2,128)S(1)}, s32[1,1,2,1024]{3,2,1,0:T(2,128)}, u32[]{:S(2)}) copy-start(s32[1,1,2,1024]{3,2,1,0:T(2,128)} %param.12) | copy-start | bytes 24580
  1.3 15.7 %all-to-all-start = ((s32[16,1,16]{2,1,0:T(1,128)}), s32[16,1,16]{2,1,0:T(1,128)S(1)}, u32[]{:S(2)}, u32[]{:S(2)}) async-start(s32[16,1,16]{2,1,0:T(1,128)} %broadcast_in_dim.6), calls=%async_computation | async-start | bytes 16384 | tf_op jit(solution)/shard_map/all_to_all | solution.py:385
  17.0 5.4 %collective-permute-start = (bf16[4,128,1024]{2,1,0:T(8,128)(2,1)}, bf16[4,128,1024]{2,1,0:T(8,128)(2,1)S(1)}, u32[]{:S(2)}, u32[]{:S(2)}) collective-permute-start(bf16[4,128,1024]{2,1,0:T(8,128)(2,1)} %sort_leaves.1.leaves_ref.refs_0_), channel_id=1, source_target_pairs={{0,1},{1,0},{2,3},{3,2},{4,5},{5,4},{6,7},{7,6},{8,9},{9,8},{10,11... | collective-permute-start | bytes 3145736 | tf_op jit(solution)/shard_map/ppermute | solution.py:365
  19.1 27.6 %collective-permute-start.1 = (bf16[4,128,1024]{2,1,0:T(8,128)(2,1)}, bf16[4,128,1024]{2,1,0:T(8,128)(2,1)}, u32[]{:S(2)}, u32[]{:S(2)}) collective-permute-start(bf16[4,128,1024]{2,1,0:T(8,128)(2,1)} %sort_leaves.1.leaves_ref.refs_0_), channel_id=1, source_target_pairs={{0,2},{1,15},{2,4},{3,1},{4,6},{5,3},{6,8},{7,5},{8,10},{9,7},{10,... | collective-permute-start | bytes 3145736 | tf_op jit(solution)/shard_map/ppermute | solution.py:370
  22.5 13.9 %copy-start.4 = (bf16[4,128,1024]{2,1,0:T(8,128)(2,1)}, bf16[4,128,1024]{2,1,0:T(8,128)(2,1)S(1)}, u32[]{:S(2)}) copy-start(bf16[4,128,1024]{2,1,0:T(8,128)(2,1)S(1)} %collective-permute-done.refs_1_) | copy-start | bytes 3145732
  22.5 26.9 %collective-permute-start.2 = (bf16[4,128,1024]{2,1,0:T(8,128)(2,1)S(1)}, bf16[4,128,1024]{2,1,0:T(8,128)(2,1)}, u32[]{:S(2)}, u32[]{:S(2)}) collective-permute-start(bf16[4,128,1024]{2,1,0:T(8,128)(2,1)S(1)} %collective-permute-done.refs_1_), channel_id=1, source_target_pairs={{0,2},{1,15},{2,4},{3,1},{4,6},{5,3},{6,8},{7,5},{8,10},{9,7},{10,... | collective-permute-start | bytes 3145736 | tf_op jit(solution)/shard_map/ppermute | solution.py:370
  27.8 1.2 copy-start
  35.2 16.7 %copy-start.1 = (bf16[4,128,1024]{2,1,0:T(8,128)(2,1)S(1)}, bf16[4,128,1024]{2,1,0:T(8,128)(2,1)}, u32[]{:S(2)}) copy-start(bf16[4,128,1024]{2,1,0:T(8,128)(2,1)} %sort_leaves.1.leaves_ref.refs_0_) | copy-start | bytes 3145732
  36.4 46.1 %all-to-all-start.1 = ((bf16[8,144,512]{2,1,0:T(8,128)(2,1)}), bf16[8,144,512]{2,1,0:T(8,128)(2,1)}, u32[]{:S(2)}, u32[]{:S(2)}) async-start(bf16[8,144,512]{2,1,0:T(8,128)(2,1)} %broadcast_in_dim.7), calls=%async_computation.1 | async-start | bytes 2359296 | tf_op jit(solution)/shard_map/all_to_all | solution.py:393
  46.7 6.8 %copy-start.6 = (s32[1,1,16,1]{2,3,1,0:T(1,128)S(1)}, s32[1,1,16,1]{2,3,1,0:T(1,128)}, u32[]{:S(2)}) copy-start(s32[1,1,16,1]{2,3,1,0:T(1,128)} %param.15) | copy-start | bytes 196
  46.7 6.8 %copy-start.7 = (s32[1,1,16,1]{2,3,1,0:T(1,128)S(1)}, s32[1,1,16,1]{2,3,1,0:T(1,128)}, u32[]{:S(2)}) copy-start(s32[1,1,16,1]{2,3,1,0:T(1,128)} %param.14) | copy-start | bytes 196
  46.7 17.0 %collective-permute-start.4 = (bf16[4,128,1024]{2,1,0:T(8,128)(2,1)}, bf16[4,128,1024]{2,1,0:T(8,128)(2,1)}, u32[]{:S(2)}, u32[]{:S(2)}) collective-permute-start(bf16[4,128,1024]{2,1,0:T(8,128)(2,1)} %collective-permute-done.1.refs_2_.refs_0_), channel_id=1, source_target_pairs={{0,2},{1,15},{2,4},{3,1},{4,6},{5,3},{6,8},{7,5},{8,10},{9,7},{10,... | collective-permute-start | bytes 3145736 | tf_op jit(solution)/shard_map/ppermute | solution.py:370
  49.4 25.6 %collective-permute-start.3 = (bf16[4,128,1024]{2,1,0:T(8,128)(2,1)}, bf16[4,128,1024]{2,1,0:T(8,128)(2,1)}, u32[]{:S(2)}, u32[]{:S(2)}) collective-permute-start(bf16[4,128,1024]{2,1,0:T(8,128)(2,1)} %collective-permute-done.2.refs_3_.refs_1_), channel_id=1, source_target_pairs={{0,2},{1,15},{2,4},{3,1},{4,6},{5,3},{6,8},{7,5},{8,10},{9,7},{10,... | collective-permute-start | bytes 3145736 | tf_op jit(solution)/shard_map/ppermute | solution.py:370
  51.9 1.6 %copy-start.5 = (bf16[4,128,1024]{2,1,0:T(8,128)(2,1)S(1)}, bf16[4,128,1024]{2,1,0:T(8,128)(2,1)}, u32[]{:S(2)}) copy-start(bf16[4,128,1024]{2,1,0:T(8,128)(2,1)} %copy-done.4) | copy-start | bytes 3145732
  55.7 1.3 %copy-start.2 = (f32[4096,128]{1,0:T(8,128)}, f32[4096,128]{1,0:T(8,128)S(1)}, u32[]{:S(2)}) copy-start(f32[4096,128]{1,0:T(8,128)S(1)} %near_terms.3.before_ref) | copy-start | bytes 6291460
  57.1 23.3 %copy-start.10 = (s32[1,1,4,3]{2,1,3,0:T(1,128)S(1)}, s32[1,1,4,3]{2,1,3,0:T(1,128)}, u32[]{:S(2)}) copy-start(s32[1,1,4,3]{2,1,3,0:T(1,128)} %param.13) | copy-start | bytes 148
  66.7 1.0 copy-start.8
  67.7 31.3 %collective-permute-start.5 = (bf16[3,128,1024]{2,1,0:T(8,128)(2,1)}, bf16[3,128,1024]{2,1,0:T(8,128)(2,1)}, u32[]{:S(2)}, u32[]{:S(2)}) collective-permute-start(bf16[3,128,1024]{2,1,0:T(8,128)(2,1)} %get-tuple-element.25), channel_id=1, source_target_pairs={{0,2},{1,15},{2,4},{3,1},{4,6},{5,3},{6,8},{7,5},{8,10},{9,7},{10,... | collective-permute-start | bytes 2359304 | tf_op jit(solution)/shard_map/ppermute | solution.py:370
  77.7 21.3 %collective-permute-start.6 = (bf16[3,128,1024]{2,1,0:T(8,128)(2,1)}, bf16[3,128,1024]{2,1,0:T(8,128)(2,1)}, u32[]{:S(2)}, u32[]{:S(2)}) collective-permute-start(bf16[3,128,1024]{2,1,0:T(8,128)(2,1)} %copy_leaves.4), channel_id=1, source_target_pairs={{0,2},{1,15},{2,4},{3,1},{4,6},{5,3},{6,8},{7,5},{8,10},{9,7},{10,... | collective-permute-start | bytes 2359304 | tf_op jit(solution)/shard_map/ppermute | solution.py:370
  80.6 29.3 %collective-permute-start.7 = (bf16[3,128,1024]{2,1,0:T(8,128)(2,1)}, bf16[3,128,1024]{2,1,0:T(8,128)(2,1)S(1)}, u32[]{:S(2)}, u32[]{:S(2)}) collective-permute-start(bf16[3,128,1024]{2,1,0:T(8,128)(2,1)} %copy-done.8), channel_id=1, source_target_pairs={{0,1},{1,0},{2,3},{3,2},{4,5},{5,4},{6,7},{7,6},{8,9},{9,8},{10,11... | collective-permute-start | bytes 2359304 | tf_op jit(solution)/shard_map/ppermute | solution.py:365
  82.5 1.6 %copy-start.3 = (f32[4096,128]{1,0:T(8,128)S(1)}, f32[4096,128]{1,0:T(8,128)}, u32[]{:S(2)}) copy-start(f32[4096,128]{1,0:T(8,128)} %copy-done.2) | copy-start | bytes 6291460
  101.0 17.1 %collective-permute-start.8 = (bf16[3,128,1024]{2,1,0:T(8,128)(2,1)S(1)}, bf16[3,128,1024]{2,1,0:T(8,128)(2,1)S(1)}, u32[]{:S(2)}, u32[]{:S(2)}) collective-permute-start(bf16[3,128,1024]{2,1,0:T(8,128)(2,1)S(1)} %get-tuple-element.32), channel_id=1, source_target_pairs={{0,1},{1,0},{2,3},{3,2},{4,5},{5,4},{6,7},{7,6},{8,9},{9,8},{10,11... | collective-permute-start | bytes 2359304 | tf_op jit(solution)/shard_map/ppermute | solution.py:365
  106.2 11.8 %collective-permute-start.9 = (bf16[2,128,1024]{2,1,0:T(8,128)(2,1)S(1)}, bf16[2,128,1024]{2,1,0:T(8,128)(2,1)S(1)}, u32[]{:S(2)}, u32[]{:S(2)}) collective-permute-start(bf16[2,128,1024]{2,1,0:T(8,128)(2,1)S(1)} %get-tuple-element.29), channel_id=1, source_target_pairs={{0,2},{1,15},{2,4},{3,1},{4,6},{5,3},{6,8},{7,5},{8,10},{9,7},{10,... | collective-permute-start | bytes 1572872 | tf_op jit(solution)/shard_map/ppermute | solution.py:370
where the time goes:
time: 128 us; the launch traced here: 126 us
  Pallas kernels  56.4 us (44%)
  starting transfers between devices  49 us (38%)
  waiting for transfers between devices  11.3 us (9%)
  local copies, waits for them, and re-layouts  8.41 us (7%)
    ppermute x7, starting transfers between devices, hop(): return lax.ppermute(value, 'task', pairs)  22.1 us
    pallas_call x3, Pallas kernels, near_terms(): pl.pallas_call(functools.partial(near_kernel, plan, first, last), out_sha...  17.8 us
    pallas_call x1, Pallas kernels, far_terms(): pl.pallas_call(far_kernel, out_shape=jax.ShapeDtypeStruct((PTS, 2 * F), j...  14.9 us
    ppermute x7, waiting for transfers between devices, hop(): return lax.ppermute(value, 'task', pairs)  11.3 us
    all_to_all x1, starting transfers between devices, body(): lax.all_to_all(jnp.broadcast_to(node, (8,) + node.shape), 'leaf', split_a...  10.3 us
    ppermute x3, starting transfers between devices, partner(): return lax.ppermute(value, axis, pairs)  9.18 us
    pallas_call x1, Pallas kernels, sort_leaves(): pl.pallas_call(sort_kernel, out_shape=jax.ShapeDtypeStruct((LEAF_DEV, 2 *...  8.27 us
    pallas_call x3, Pallas kernels, copy_leaves(): pl.pallas_call(functools.partial(copy_kernel, picks), out_shape=[jax.Shap...  7.67 us
  transfers between devices with their start and end apart: 12, of which 2 were waited for; matrix products, arithmetic and copies ran while one was open for 2% of the time, Pallas kernels for 39%

commit v1 on v0

--- a/solution.py
+++ b/solution.py
@@ -409,29 +409,29 @@
         ],
     )
     two_a = after(two_a, total)
+    [send] = copy_leaves(
+        me, table, [two_a], [[(0, asked(2, 0, 1, 0)), (0, asked(2, 0, 1, 1)), (0, asked(2, 0, 2, 0))]]
+    )
+    three_a = hop(send)
+    two_b = after(two_b, send)
     send, send_side = copy_leaves(
         me,
         table,
-        [one_a, one_b, two_a],
+        [one_a, one_b, two_a, two_b],
         [
-            [(2, asked(2, 0, 1, 0)), (2, asked(2, 0, 1, 1)), (2, asked(2, 0, 2, 0))],
-            [(0, asked(1, 0, 0, 1)), (1, asked(1, 1, 0, 1)), (2, asked(2, 0, 0, 1))],
-        ],
-    )
-    three_a = hop(send)
+            [(3, asked(2, 1, 1, 0)), (3, asked(2, 1, 1, 1)), (3, asked(2, 1, 2, 0))],
+            [(0, asked(1, 0, 0, 1)), (1, asked(1, 1, 0, 1)), (2, asked(2, 0, 0, 1)), (3, asked(2, 1, 0, 1))],
+        ],
+    )
+    three_b = hop(send)
     side = partner(send_side, "task", 0)
-    two_b = after(two_b, send)
-    [send] = copy_leaves(
-        me, table, [two_b], [[(0, asked(2, 1, 1, 0)), (0, asked(2, 1, 1, 1)), (0, asked(2, 1, 2, 0))]]
-    )
-    three_b = hop(send)
     total = far_terms(place, far_list.reshape(-1), left, total, after(nodes, send))
     three_a = after(three_a, total)
     send, send_side = copy_leaves(
         me,
         table,
-        [two_b, three_a, three_b],
-        [[(1, at_slot(2)), (2, at_slot(2))], [(0, asked(2, 1, 0, 1)), (1, at_slot(1)), (2, at_slot(1))]],
+        [three_a, three_b],
+        [[(0, at_slot(2)), (1, at_slot(2))], [(0, at_slot(1)), (1, at_slot(1))]],
     )
     four = hop(send)
     last_side = partner(send_side, "task", 0)
@@ -444,20 +444,21 @@
             (side, -1, 1, 0),
             (side, -1, 0, 1),
             (side, -2, 1, 2),
+            (side, -2, 0, 3),
             (three_a, 3, 0, 0),
             (three_b, 3, 1, 0),
         ],
     )
-    last_side = after(last_side, total)
+    four = after(four, total)
+    last_side = after(last_side, four)
     total = near(
         left,
         total,
         [
-            (last_side, -2, 0, 0),
-            (last_side, -3, 1, 1),
-            (last_side, -3, 0, 2),
-            (after(four, last_side), 4, 0, 0),
+            (four, 4, 0, 0),
             (four, 4, 1, 1),
+            (last_side, -3, 1, 0),
+            (last_side, -3, 0, 1),
         ],
         last=True,
     )

time: 128 us -> 128 us (level)
  the two profiles are of different devices: /device:TPU:22 before, /device:TPU:195 now
where the time goes in v1:
time: 128 us; the launch traced here: 127 us
  Pallas kernels  65.9 us (51%)
  starting transfers between devices  48.9 us (38%)
  local copies, waits for them, and re-layouts  7.46 us (6%)
  waiting for transfers between devices  4.22 us (3%)
    ppermute x7, starting transfers between devices, hop(): return lax.ppermute(value, 'task', pairs)  27.2 us
    pallas_call x3, Pallas kernels, near_terms(): pl.pallas_call(functools.partial(near_kernel, plan, first, last), out_sha...  24.1 us
    pallas_call x1, Pallas kernels, far_terms(): pl.pallas_call(far_kernel, out_shape=jax.ShapeDtypeStruct((PTS, 2 * F), j...  17.7 us
    pallas_call x1, Pallas kernels, sort_leaves(): pl.pallas_call(sort_kernel, out_shape=jax.ShapeDtypeStruct((LEAF_DEV, 2 *...  8.27 us
    pallas_call x3, Pallas kernels, copy_leaves(): pl.pallas_call(functools.partial(copy_kernel, picks), out_shape=[jax.Shap...  8 us
    all_to_all x1, starting transfers between devices, body(): table = lax.all_to_all(row, 'task', split_axis=0, concat_axis=0, tiled=True)  7.79 us
    all_to_all x1, starting transfers between devices, body(): lax.all_to_all(jnp.broadcast_to(node, (8,) + node.shape), 'leaf', split_a...  7.59 us
    ppermute x3, starting transfers between devices, partner(): return lax.ppermute(value, axis, pairs)  6.3 us
  transfers between devices with their start and end apart: 12, of which 1 were waited for; matrix products, arithmetic and copies ran while one was open for 2% of the time, Pallas kernels for 47%

profile of v1, /device:TPU:195, one launch (start us, length us, event | category | flops | bytes accessed | tf_op | source)
XLA Modules:
  0.0 126.9 jit_solution(4776110166551010738)
XLA Ops:
  0.0 1.3 %broadcast_in_dim.6 = s32[16,1,16]{2,1,0:T(1,128)} broadcast(s32[16]{0:T(128)} %bitcast.11), dimensions={2} | broadcast | bytes 1088 | tf_op jit(solution)/shard_map/broadcast_in_dim | solution.py:384
  1.3 7.8 %all-to-all-start = ((s32[16,1,16]{2,1,0:T(1,128)}), s32[16,1,16]{2,1,0:T(1,128)S(1)}, u32[]{:S(2)}, u32[]{:S(2)}) async-start(s32[16,1,16]{2,1,0:T(1,128)} %broadcast_in_dim.6), calls=%async_computation | async-start | bytes 16384 | tf_op jit(solution)/shard_map/all_to_all | solution.py:385
  9.1 8.3 %sort_leaves.1.leaves_ref.refs_0_ = bf16[4,128,1024]{2,1,0:T(8,128)(2,1)} custom-call(s32[4096]{0:T(1024)} %bitcast.20, bf16[64,4096]{1,0:T(8,128)(2,1)} %bitcast.18, bf16[64,4096]{1,0:T(8,128)(2,1)} %bitcast.19), custom_call_target="tpu_custom_call" | custom-call | bytes 1000 | tf_op jit(solution)/shard_map/sort_leaves/pallas_call | solution.py:63
  17.4 2.0 %collective-permute-start = (bf16[4,128,1024]{2,1,0:T(8,128)(2,1)}, bf16[4,128,1024]{2,1,0:T(8,128)(2,1)S(1)}, u32[]{:S(2)}, u32[]{:S(2)}) collective-permute-start(bf16[4,128,1024]{2,1,0:T(8,128)(2,1)} %sort_leaves.1.leaves_ref.refs_0_), channel_id=1, source_target_pairs={{0,1},{1,0},{2,3},{3,2},{4,5},{5,4},{6,7},{7,6},{8,9},{9,8},{10,11... | collective-permute-start | bytes 3145736 | tf_op jit(solution)/shard_map/ppermute | solution.py:365
  19.4 4.8 %collective-permute-start.1 = (bf16[4,128,1024]{2,1,0:T(8,128)(2,1)}, bf16[4,128,1024]{2,1,0:T(8,128)(2,1)}, u32[]{:S(2)}, u32[]{:S(2)}) collective-permute-start(bf16[4,128,1024]{2,1,0:T(8,128)(2,1)} %sort_leaves.1.leaves_ref.refs_0_), channel_id=1, source_target_pairs={{0,2},{1,15},{2,4},{3,1},{4,6},{5,3},{6,8},{7,5},{8,10},{9,7},{10,... | collective-permute-start | bytes 3145736 | tf_op jit(solution)/shard_map/ppermute | solution.py:370
  24.2 3.1 %collective-permute-start.2 = (bf16[4,128,1024]{2,1,0:T(8,128)(2,1)S(1)}, bf16[4,128,1024]{2,1,0:T(8,128)(2,1)}, u32[]{:S(2)}, u32[]{:S(2)}) collective-permute-start(bf16[4,128,1024]{2,1,0:T(8,128)(2,1)S(1)} %collective-permute-done.refs_1_), channel_id=1, source_target_pairs={{0,2},{1,15},{2,4},{3,1},{4,6},{5,3},{6,8},{7,5},{8,10},{9,7},{10,... | collective-permute-start | bytes 3145736 | tf_op jit(solution)/shard_map/ppermute | solution.py:370
  27.3 0.7 slice.8.index_ref
  28.0 1.2 copy-done
  29.2 6.2 %first_node.1 = bf16[144,512]{1,0:T(8,128)(2,1)S(1)} custom-call(s32[1,512]{1,0:T(1,128)S(1)} %slice.8.index_ref, s32[2,512]{1,0:T(2,128)S(1)} %slice_bitcast_fusion.merge_ref, bf16[4,128,1024]{2,1,0:T(8,128)(2,1)S(1)} %copy-done), custom_call_target="tpu_custom_call" | custom-call | bytes 1000 | tf_op jit(solution)/shard_map/first_node/pallas_call | solution.py:179
  35.4 0.0 copy-start.1
  35.4 1.1 broadcast_in_dim.7
  36.6 7.6 %all-to-all-start.1 = ((bf16[8,144,512]{2,1,0:T(8,128)(2,1)}), bf16[8,144,512]{2,1,0:T(8,128)(2,1)}, u32[]{:S(2)}, u32[]{:S(2)}) async-start(bf16[8,144,512]{2,1,0:T(8,128)(2,1)} %broadcast_in_dim.7), calls=%async_computation.1 | async-start | bytes 2359296 | tf_op jit(solution)/shard_map/all_to_all | solution.py:393
  44.2 3.2 %collective-permute-start.3 = (bf16[4,128,1024]{2,1,0:T(8,128)(2,1)}, bf16[4,128,1024]{2,1,0:T(8,128)(2,1)}, u32[]{:S(2)}, u32[]{:S(2)}) collective-permute-start(bf16[4,128,1024]{2,1,0:T(8,128)(2,1)} %collective-permute-done.1.refs_2_.refs_0_), channel_id=1, source_target_pairs={{0,2},{1,15},{2,4},{3,1},{4,6},{5,3},{6,8},{7,5},{8,10},{9,7},{10,... | collective-permute-start | bytes 3145736 | tf_op jit(solution)/shard_map/ppermute | solution.py:370
  47.4 5.3 %collective-permute-start.4 = (bf16[4,128,1024]{2,1,0:T(8,128)(2,1)}, bf16[4,128,1024]{2,1,0:T(8,128)(2,1)}, u32[]{:S(2)}, u32[]{:S(2)}) collective-permute-start(bf16[4,128,1024]{2,1,0:T(8,128)(2,1)} %collective-permute-done.2.refs_3_.refs_1_), channel_id=1, source_target_pairs={{0,2},{1,15},{2,4},{3,1},{4,6},{5,3},{6,8},{7,5},{8,10},{9,7},{10,... | collective-permute-start | bytes 3145736 | tf_op jit(solution)/shard_map/ppermute | solution.py:370
  52.8 1.6 %target_factors.1.left_ref = bf16[4096,256]{1,0:T(8,128)(2,1)S(1)} custom-call(bf16[4,128,1024]{2,1,0:T(8,128)(2,1)S(1)} %copy-done.1), custom_call_target="tpu_custom_call" | custom-call | bytes 1000 | tf_op jit(solution)/shard_map/target_factors/pallas_call | solution.py:122
  54.4 6.0 %near_terms.3.before_ref = f32[4096,128]{1,0:T(8,128)S(1)} custom-call(s32[1]{0:T(128)} %bitcast.me_ref, s32[16]{0:T(128)S(1)} %bitcast.12, s32[16]{0:T(128)S(1)} %bitcast.15, bf16[4096,256]{1,0:T(8,128)(2,1)S(1)} %target_factors.1.left_ref, bf16[4,128,1024]{2,1,0:T(8,128)(2,1)S(1)} %copy-done.1, bf16[4,128,1024]{2,1,0:T(8,128)(2,1)S(1)} %copy-done.5, ...), custom_call_target="tpu_custom_call" | custom-call | bytes 1000 | tf_op jit(solution)/shard_map/near_terms/pallas_call | solution.py:351
  60.4 1.3 %copy-done.2 = f32[4096,128]{1,0:T(8,128)} copy-done((f32[4096,128]{1,0:T(8,128)}, f32[4096,128]{1,0:T(8,128)S(1)}, u32[]{:S(2)}) %copy-start.2) | copy-done | bytes 2097176
  61.7 2.7 %copy_leaves.3 = bf16[3,128,1024]{2,1,0:T(8,128)(2,1)} custom-call(s32[1]{0:T(128)} %bitcast.me_ref, s32[16,1,16]{2,1,0:T(1,128)S(1)} %all-to-all-done.table_ref, bf16[4,128,1024]{2,1,0:T(8,128)(2,1)} %collective-permute-done.3.refs_0_.refs_2_.refs_1_), custom_call_target="tpu_custom_call" | custom-call | bytes 1000 | tf_op jit(solution)/shard_map/copy_leaves/pallas_call | solution.py:288
  64.5 3.0 %collective-permute-start.5 = (bf16[3,128,1024]{2,1,0:T(8,128)(2,1)}, bf16[3,128,1024]{2,1,0:T(8,128)(2,1)}, u32[]{:S(2)}, u32[]{:S(2)}) collective-permute-start(bf16[3,128,1024]{2,1,0:T(8,128)(2,1)} %copy_leaves.3), channel_id=1, source_target_pairs={{0,2},{1,15},{2,4},{3,1},{4,6},{5,3},{6,8},{7,5},{8,10},{9,7},{10,... | collective-permute-start | bytes 2359304 | tf_op jit(solution)/shard_map/ppermute | solution.py:370
  67.5 4.2 %collective-permute-done.4.refs_3_.refs_2_ = bf16[4,128,1024]{2,1,0:T(8,128)(2,1)} collective-permute-done((bf16[4,128,1024]{2,1,0:T(8,128)(2,1)}, bf16[4,128,1024]{2,1,0:T(8,128)(2,1)}, u32[]{:S(2)}, u32[]{:S(2)}) %collective-permute-start.4) | collective-permute-done | bytes 1048608 | tf_op jit(solution)/shard_map/ppermute | solution.py:370
  71.7 3.4 %copy_leaves.4 = (bf16[3,128,1024]{2,1,0:T(8,128)(2,1)}, bf16[4,128,1024]{2,1,0:T(8,128)(2,1)}) custom-call(s32[1]{0:T(128)} %bitcast.me_ref, s32[16,1,16]{2,1,0:T(1,128)S(1)} %all-to-all-done.table_ref, bf16[4,128,1024]{2,1,0:T(8,128)(2,1)} %collective-permute-done.1.refs_2_.refs_0_, bf16[4,128,1024]{2,1,0:T(8,128)(2,1)} %collective-permute-done.2.refs_3_.refs_1_, ...), custom_call_target="tpu_custom_call" | custom-call | bytes 1000 | tf_op jit(solution)/shard_map/copy_leaves/pallas_call | solution.py:288
  75.1 4.0 %collective-permute-start.6 = (bf16[3,128,1024]{2,1,0:T(8,128)(2,1)}, bf16[3,128,1024]{2,1,0:T(8,128)(2,1)}, u32[]{:S(2)}, u32[]{:S(2)}) collective-permute-start(bf16[3,128,1024]{2,1,0:T(8,128)(2,1)} %get-tuple-element.26), channel_id=1, source_target_pairs={{0,2},{1,15},{2,4},{3,1},{4,6},{5,3},{6,8},{7,5},{8,10},{9,7},{10,... | collective-permute-start | bytes 2359304 | tf_op jit(solution)/shard_map/ppermute | solution.py:370
  79.1 2.4 %collective-permute-start.7 = (bf16[4,128,1024]{2,1,0:T(8,128)(2,1)}, bf16[4,128,1024]{2,1,0:T(8,128)(2,1)S(1)}, u32[]{:S(2)}, u32[]{:S(2)}) collective-permute-start(bf16[4,128,1024]{2,1,0:T(8,128)(2,1)} %get-tuple-element.31), channel_id=1, source_target_pairs={{0,1},{1,0},{2,3},{3,2},{4,5},{5,4},{6,7},{7,6},{8,9},{9,8},{10,11... | collective-permute-start | bytes 3145736 | tf_op jit(solution)/shard_map/ppermute | solution.py:365
  81.5 0.1 copy.10
  81.6 0.1 reshape.26.flags_ref
  81.7 1.6 %copy-done.3 = f32[4096,128]{1,0:T(8,128)S(1)} copy-done((f32[4096,128]{1,0:T(8,128)S(1)}, f32[4096,128]{1,0:T(8,128)}, u32[]{:S(2)}) %copy-start.3) | copy-done | bytes 2097176
  83.3 17.7 %far_terms.1.refs_0_ = f32[4096,128]{1,0:T(8,128)S(1)} custom-call(s32[1]{0:T(128)} %bitcast.6.place_ref, s32[12]{0:T(128)S(1)} %reshape.26.flags_ref, bf16[4096,256]{1,0:T(8,128)(2,1)S(1)} %target_factors.1.left_ref, f32[4096,128]{1,0:T(8,128)S(1)} %copy-done.3, bf16[8,144,512]{2,1,0:T(8,128)(2,1)} %all-to-all-done.1.nodes_ref), custom_call_target="tpu_custom_call" | custom-call | bytes 1000 | tf_op jit(solution)/shard_map/far_terms/pallas_call | solution.py:249
  101.0 1.9 %copy_leaves.5 = (bf16[2,128,1024]{2,1,0:T(8,128)(2,1)S(1)}, bf16[2,128,1024]{2,1,0:T(8,128)(2,1)S(1)}) custom-call(s32[1]{0:T(128)} %bitcast.me_ref, s32[16,1,16]{2,1,0:T(1,128)S(1)} %all-to-all-done.table_ref, bf16[3,128,1024]{2,1,0:T(8,128)(2,1)} %collective-permute-done.5.refs_0_.refs_7_, bf16[3,128,1024]{2,1,0:T(8,128)(2,1)} %collective-permute-done.6.refs_1_.refs_8_), custom_call_target="tpu_custom_call" | custom-call | bytes 1000 | tf_op jit(solution)/shard_map/copy_leaves/pallas_call | solution.py:288
  102.9 3.7 %collective-permute-start.8 = (bf16[2,128,1024]{2,1,0:T(8,128)(2,1)S(1)}, bf16[2,128,1024]{2,1,0:T(8,128)(2,1)S(1)}, u32[]{:S(2)}, u32[]{:S(2)}) collective-permute-start(bf16[2,128,1024]{2,1,0:T(8,128)(2,1)S(1)} %get-tuple-element.29), channel_id=1, source_target_pairs={{0,2},{1,15},{2,4},{3,1},{4,6},{5,3},{6,8},{7,5},{8,10},{9,7},{10,... | collective-permute-start | bytes 1572872 | tf_op jit(solution)/shard_map/ppermute | solution.py:370
  106.6 1.9 %collective-permute-start.9 = (bf16[2,128,1024]{2,1,0:T(8,128)(2,1)S(1)}, bf16[2,128,1024]{2,1,0:T(8,128)(2,1)S(1)}, u32[]{:S(2)}, u32[]{:S(2)}) collective-permute-start(bf16[2,128,1024]{2,1,0:T(8,128)(2,1)S(1)} %get-tuple-element.33), channel_id=1, source_target_pairs={{0,1},{1,0},{2,3},{3,2},{4,5},{5,4},{6,7},{7,6},{8,9},{9,8},{10,11... | collective-permute-start | bytes 1572872 | tf_op jit(solution)/shard_map/ppermute | solution.py:365
  108.6 11.9 %near_terms.4.refs_0_ = f32[4096,128]{1,0:T(8,128)S(1)} custom-call(s32[1]{0:T(128)} %bitcast.me_ref, s32[16]{0:T(128)S(1)} %bitcast.13, s32[16]{0:T(128)S(1)} %bitcast.16, bf16[4096,256]{1,0:T(8,128)(2,1)S(1)} %target_factors.1.left_ref, f32[4096,128]{1,0:T(8,128)S(1)} %far_terms.1.refs_0_, ...), custom_call_target="tpu_custom_call" | custom-call | bytes 1000 | tf_op jit(solution)/shard_map/near_terms/pallas_call | solution.py:351
  120.5 6.2 %near_terms.5 = f32[64,4096]{1,0:T(8,128)} custom-call(s32[1]{0:T(128)} %bitcast.me_ref, s32[16]{0:T(128)S(1)} %bitcast.14, s32[16]{0:T(128)S(1)} %bitcast.17, bf16[4096,256]{1,0:T(8,128)(2,1)S(1)} %target_factors.1.left_ref, f32[4096,128]{1,0:T(8,128)S(1)} %near_terms.4.refs_0_, bf16[2,128,1024]{2,1,0:T(8,128)(2,1)S(1)} %collective-permute-done.8.refs_1_.refs_2_, ...), custom_call_target="tpu_custom_call" | custom-call | bytes 1000 | tf_op jit(solution)/shard_map/near_terms/pallas_call | solution.py:351
  (28 shorter events, 0.1 us)
Async XLA Ops:
  0.0 28.0 %copy-start.8 = (s32[1,1,2,1024]{3,2,1,0:T(2,128)S(1)}, s32[1,1,2,1024]{3,2,1,0:T(2,128)}, u32[]{:S(2)}) copy-start(s32[1,1,2,1024]{3,2,1,0:T(2,128)} %param.12) | copy-start | bytes 24580
  1.3 16.1 %all-to-all-start = ((s32[16,1,16]{2,1,0:T(1,128)}), s32[16,1,16]{2,1,0:T(1,128)S(1)}, u32[]{:S(2)}, u32[]{:S(2)}) async-start(s32[16,1,16]{2,1,0:T(1,128)} %broadcast_in_dim.6), calls=%async_computation | async-start | bytes 16384 | tf_op jit(solution)/shard_map/all_to_all | solution.py:385
  17.4 6.8 %collective-permute-start = (bf16[4,128,1024]{2,1,0:T(8,128)(2,1)}, bf16[4,128,1024]{2,1,0:T(8,128)(2,1)S(1)}, u32[]{:S(2)}, u32[]{:S(2)}) collective-permute-start(bf16[4,128,1024]{2,1,0:T(8,128)(2,1)} %sort_leaves.1.leaves_ref.refs_0_), channel_id=1, source_target_pairs={{0,1},{1,0},{2,3},{3,2},{4,5},{5,4},{6,7},{7,6},{8,9},{9,8},{10,11... | collective-permute-start | bytes 3145736 | tf_op jit(solution)/shard_map/ppermute | solution.py:365
  19.4 24.8 %collective-permute-start.1 = (bf16[4,128,1024]{2,1,0:T(8,128)(2,1)}, bf16[4,128,1024]{2,1,0:T(8,128)(2,1)}, u32[]{:S(2)}, u32[]{:S(2)}) collective-permute-start(bf16[4,128,1024]{2,1,0:T(8,128)(2,1)} %sort_leaves.1.leaves_ref.refs_0_), channel_id=1, source_target_pairs={{0,2},{1,15},{2,4},{3,1},{4,6},{5,3},{6,8},{7,5},{8,10},{9,7},{10,... | collective-permute-start | bytes 3145736 | tf_op jit(solution)/shard_map/ppermute | solution.py:370
  24.2 12.4 %copy-start.4 = (bf16[4,128,1024]{2,1,0:T(8,128)(2,1)}, bf16[4,128,1024]{2,1,0:T(8,128)(2,1)S(1)}, u32[]{:S(2)}) copy-start(bf16[4,128,1024]{2,1,0:T(8,128)(2,1)S(1)} %collective-permute-done.refs_1_) | copy-start | bytes 3145732
  24.2 23.3 %collective-permute-start.2 = (bf16[4,128,1024]{2,1,0:T(8,128)(2,1)S(1)}, bf16[4,128,1024]{2,1,0:T(8,128)(2,1)}, u32[]{:S(2)}, u32[]{:S(2)}) collective-permute-start(bf16[4,128,1024]{2,1,0:T(8,128)(2,1)S(1)} %collective-permute-done.refs_1_), channel_id=1, source_target_pairs={{0,2},{1,15},{2,4},{3,1},{4,6},{5,3},{6,8},{7,5},{8,10},{9,7},{10,... | collective-permute-start | bytes 3145736 | tf_op jit(solution)/shard_map/ppermute | solution.py:370
  28.0 1.2 copy-start
  35.4 17.3 %copy-start.1 = (bf16[4,128,1024]{2,1,0:T(8,128)(2,1)S(1)}, bf16[4,128,1024]{2,1,0:T(8,128)(2,1)}, u32[]{:S(2)}) copy-start(bf16[4,128,1024]{2,1,0:T(8,128)(2,1)} %sort_leaves.1.leaves_ref.refs_0_) | copy-start | bytes 3145732
  36.6 45.1 %all-to-all-start.1 = ((bf16[8,144,512]{2,1,0:T(8,128)(2,1)}), bf16[8,144,512]{2,1,0:T(8,128)(2,1)}, u32[]{:S(2)}, u32[]{:S(2)}) async-start(bf16[8,144,512]{2,1,0:T(8,128)(2,1)} %broadcast_in_dim.7), calls=%async_computation.1 | async-start | bytes 2359296 | tf_op jit(solution)/shard_map/all_to_all | solution.py:393
  44.2 10.2 %copy-start.6 = (s32[1,1,16,1]{2,3,1,0:T(1,128)S(1)}, s32[1,1,16,1]{2,3,1,0:T(1,128)}, u32[]{:S(2)}) copy-start(s32[1,1,16,1]{2,3,1,0:T(1,128)} %param.15) | copy-start | bytes 196
  44.2 10.2 %copy-start.7 = (s32[1,1,16,1]{2,3,1,0:T(1,128)S(1)}, s32[1,1,16,1]{2,3,1,0:T(1,128)}, u32[]{:S(2)}) copy-start(s32[1,1,16,1]{2,3,1,0:T(1,128)} %param.14) | copy-start | bytes 196
  44.2 17.6 %collective-permute-start.3 = (bf16[4,128,1024]{2,1,0:T(8,128)(2,1)}, bf16[4,128,1024]{2,1,0:T(8,128)(2,1)}, u32[]{:S(2)}, u32[]{:S(2)}) collective-permute-start(bf16[4,128,1024]{2,1,0:T(8,128)(2,1)} %collective-permute-done.1.refs_2_.refs_0_), channel_id=1, source_target_pairs={{0,2},{1,15},{2,4},{3,1},{4,6},{5,3},{6,8},{7,5},{8,10},{9,7},{10,... | collective-permute-start | bytes 3145736 | tf_op jit(solution)/shard_map/ppermute | solution.py:370
  47.4 24.3 %collective-permute-start.4 = (bf16[4,128,1024]{2,1,0:T(8,128)(2,1)}, bf16[4,128,1024]{2,1,0:T(8,128)(2,1)}, u32[]{:S(2)}, u32[]{:S(2)}) collective-permute-start(bf16[4,128,1024]{2,1,0:T(8,128)(2,1)} %collective-permute-done.2.refs_3_.refs_1_), channel_id=1, source_target_pairs={{0,2},{1,15},{2,4},{3,1},{4,6},{5,3},{6,8},{7,5},{8,10},{9,7},{10,... | collective-permute-start | bytes 3145736 | tf_op jit(solution)/shard_map/ppermute | solution.py:370
  52.8 1.6 %copy-start.5 = (bf16[4,128,1024]{2,1,0:T(8,128)(2,1)S(1)}, bf16[4,128,1024]{2,1,0:T(8,128)(2,1)}, u32[]{:S(2)}) copy-start(bf16[4,128,1024]{2,1,0:T(8,128)(2,1)} %copy-done.4) | copy-start | bytes 3145732
  60.4 1.3 %copy-start.2 = (f32[4096,128]{1,0:T(8,128)}, f32[4096,128]{1,0:T(8,128)S(1)}, u32[]{:S(2)}) copy-start(f32[4096,128]{1,0:T(8,128)S(1)} %near_terms.3.before_ref) | copy-start | bytes 6291460
  64.4 17.1 %copy-start.9 = (s32[1,1,4,3]{2,1,3,0:T(1,128)S(1)}, s32[1,1,4,3]{2,1,3,0:T(1,128)}, u32[]{:S(2)}) copy-start(s32[1,1,4,3]{2,1,3,0:T(1,128)} %param.13) | copy-start | bytes 148
  64.5 36.6 %collective-permute-start.5 = (bf16[3,128,1024]{2,1,0:T(8,128)(2,1)}, bf16[3,128,1024]{2,1,0:T(8,128)(2,1)}, u32[]{:S(2)}, u32[]{:S(2)}) collective-permute-start(bf16[3,128,1024]{2,1,0:T(8,128)(2,1)} %copy_leaves.3), channel_id=1, source_target_pairs={{0,2},{1,15},{2,4},{3,1},{4,6},{5,3},{6,8},{7,5},{8,10},{9,7},{10,... | collective-permute-start | bytes 2359304 | tf_op jit(solution)/shard_map/ppermute | solution.py:370
  75.1 25.9 %collective-permute-start.6 = (bf16[3,128,1024]{2,1,0:T(8,128)(2,1)}, bf16[3,128,1024]{2,1,0:T(8,128)(2,1)}, u32[]{:S(2)}, u32[]{:S(2)}) collective-permute-start(bf16[3,128,1024]{2,1,0:T(8,128)(2,1)} %get-tuple-element.26), channel_id=1, source_target_pairs={{0,2},{1,15},{2,4},{3,1},{4,6},{5,3},{6,8},{7,5},{8,10},{9,7},{10,... | collective-permute-start | bytes 2359304 | tf_op jit(solution)/shard_map/ppermute | solution.py:370
  79.1 29.4 %collective-permute-start.7 = (bf16[4,128,1024]{2,1,0:T(8,128)(2,1)}, bf16[4,128,1024]{2,1,0:T(8,128)(2,1)S(1)}, u32[]{:S(2)}, u32[]{:S(2)}) collective-permute-start(bf16[4,128,1024]{2,1,0:T(8,128)(2,1)} %get-tuple-element.31), channel_id=1, source_target_pairs={{0,1},{1,0},{2,3},{3,2},{4,5},{5,4},{6,7},{7,6},{8,9},{9,8},{10,11... | collective-permute-start | bytes 3145736 | tf_op jit(solution)/shard_map/ppermute | solution.py:365
  81.7 1.6 %copy-start.3 = (f32[4096,128]{1,0:T(8,128)S(1)}, f32[4096,128]{1,0:T(8,128)}, u32[]{:S(2)}) copy-start(f32[4096,128]{1,0:T(8,128)} %copy-done.2) | copy-start | bytes 6291460
  102.9 17.6 %collective-permute-start.8 = (bf16[2,128,1024]{2,1,0:T(8,128)(2,1)S(1)}, bf16[2,128,1024]{2,1,0:T(8,128)(2,1)S(1)}, u32[]{:S(2)}, u32[]{:S(2)}) collective-permute-start(bf16[2,128,1024]{2,1,0:T(8,128)(2,1)S(1)} %get-tuple-element.29), channel_id=1, source_target_pairs={{0,2},{1,15},{2,4},{3,1},{4,6},{5,3},{6,8},{7,5},{8,10},{9,7},{10,... | collective-permute-start | bytes 1572872 | tf_op jit(solution)/shard_map/ppermute | solution.py:370
  106.6 13.9 %collective-permute-start.9 = (bf16[2,128,1024]{2,1,0:T(8,128)(2,1)S(1)}, bf16[2,128,1024]{2,1,0:T(8,128)(2,1)S(1)}, u32[]{:S(2)}, u32[]{:S(2)}) collective-permute-start(bf16[2,128,1024]{2,1,0:T(8,128)(2,1)S(1)} %get-tuple-element.33), channel_id=1, source_target_pairs={{0,1},{1,0},{2,3},{3,2},{4,5},{5,4},{6,7},{7,6},{8,9},{9,8},{10,11... | collective-permute-start | bytes 1572872 | tf_op jit(solution)/shard_map/ppermute | solution.py:365
